TPU v7x, 32 devices: a whole 2x2x4 slice. The times are simulated.
32 devices in a mesh: row: 2 (over y), col: 4 (over z), rep: 4 (over x, core).
Axes of the slice: x: 2, y: 2, z: 4, core: 2. Of those that a mesh axis runs over, the one named last changes fastest.
Arguments:
- p_values: float32 [16, 4, 12, 128, 128], P(('row', 'col'), 'rep'), may hold values from -2.5 to 2.5
- p_cols: int32 [64, 12], replicated, may hold values from 0 to 63, as said below
- out_cols: int32 [64, 8], P(('row', 'col')), may hold values from 0 to 63, as said below
Outputs:
- square: float32 [64, 8, 128, 128], P(('row', 'col', 'rep'))
Inputs may be any that keep to these rules, and one draw needn't show every extreme that they name: `p_cols`: block row r names 12 distinct block columns c with r - 16 <= c < r + 16; its slots l * 3 to (l + 1) * 3 - 1 hold exactly the 3 columns that are congruent to l modulo 4. `out_cols`: block row r names 8 distinct block columns c with r - 16 <= c <= r + 16.
All inputs are finite; a program needn't handle non-finite values.
Results may differ from a plain program's by a relative error of at most 0.0003.
Values sent between devices are 32-bit elements; how exact they have to be, the bound alone decides.
A program may use at most 64 MiB of HBM per device.

v0:
```python
import jax
import jax.numpy as jnp
from jax import lax
from jax.sharding import PartitionSpec as P

HIGHEST = lax.Precision.HIGHEST


def passed_along(x, axis, by):
    peers = lax.axis_size(axis)
    pairs = [(i, i + by) for i in range(peers) if 0 <= i + by < peers]
    return lax.ppermute(x, axis, pairs)


def on_device(p_values, p_cols, out_cols):
    layers = lax.axis_size("rep")
    layer_index = lax.axis_index("rep")
    segment = lax.axis_index(("row", "col"))
    own_rows = p_values[:, 0]
    row_count = own_rows.shape[0]
    slot_total = own_rows.shape[1]
    block_size = own_rows.shape[2]
    per_layer = slot_total // layers
    seg_rows = row_count * layers
    gathered = lax.all_gather(p_values, "rep", axis=1, tiled=True)
    entries = lax.dynamic_slice_in_dim(gathered, layer_index * per_layer, per_layer, 2)
    entries = entries.reshape(seg_rows, per_layer, block_size, block_size)
    received = []
    for offset in (2, 1, -1, -2):
        received.append(passed_along(own_rows, ("row", "col"), offset))
    window_rows = jnp.concatenate(
        [received[0], received[1], own_rows, received[2], received[3]], axis=0
    )
    inner_cols = lax.dynamic_slice(
        p_cols, (segment * seg_rows, layer_index * per_layer), (seg_rows, per_layer)
    )
    far_cols = p_cols[inner_cols]
    slot_ids = jnp.arange(slot_total, dtype=jnp.int32)
    matches = far_cols[:, :, None, :] == out_cols[:, None, :, None]
    slot_index = jnp.sum(jnp.where(matches, slot_ids, 0), axis=3)
    present = jnp.any(matches, axis=3)
    window_idx = inner_cols // layers - (segment - 2) * row_count

    def one_row(row_index):
        picked = window_rows[window_idx[row_index][:, None], slot_index[row_index]]
        picked = jnp.where(present[row_index][:, :, None, None], picked, jnp.zeros_like(picked))
        return jnp.einsum("sab,sfbc->fac", entries[row_index], picked, precision=HIGHEST)

    return lax.psum_scatter(
        lax.map(one_row, jnp.arange(row_count * lax.axis_size("rep"), dtype=jnp.int32)),
        "rep",
        scatter_dimension=0,
        tiled=True,
    )


def solution(mesh):
    in_specs = (P(("row", "col"), "rep", None, None, None), P(), P(("row", "col"), None))
    out_specs = P(("row", "col", "rep"), None, None, None)
    return jax.shard_map(
        on_device, mesh=mesh, in_specs=in_specs, out_specs=out_specs, check_vma=False
    )
```

profile of v0, /device:TPU:5, one launch (start us, length us, event | category | flops | bytes accessed | tf_op | source)
XLA Modules:
  0.0 354.6 jit_solution(8983213510785722466)
XLA Ops:
  7.3 4.2 %collective-permute-start = (f32[2,12,128,128]{3,2,1,0:T(8,128)}, f32[2,12,128,128]{3,2,1,0:T(8,128)}, u32[]{:S(2)}, u32[]{:S(2)}) collective-permute-start(f32[2,12,128,128]{3,2,1,0:T(8,128)} %bitcast.41), channel_id=1, source_target_pairs={{0,8},{4,12},{8,16},{12,20},{16,24},{20,28},{1,9},{5,13},{9,17},{1... | collective-permute-start | bytes 4718600 | tf_op jit(solution)/shard_map/ppermute | solution.py:12
  11.5 3.2 collective-permute-start.1
  14.7 4.8 %collective-permute-start.2 = (f32[2,12,128,128]{3,2,1,0:T(8,128)}, f32[2,12,128,128]{3,2,1,0:T(8,128)}, u32[]{:S(2)}, u32[]{:S(2)}) collective-permute-start(f32[2,12,128,128]{3,2,1,0:T(8,128)} %bitcast.43), channel_id=1, source_target_pairs={{4,0},{8,4},{12,8},{16,12},{20,16},{24,20},{28,24},{5,1},{9,5},{13... | collective-permute-start | bytes 4718600 | tf_op jit(solution)/shard_map/ppermute | solution.py:12
  25.5 88.5 %collective-permute-done = f32[2,12,128,128]{3,2,1,0:T(8,128)} collective-permute-done((f32[2,12,128,128]{3,2,1,0:T(8,128)}, f32[2,12,128,128]{3,2,1,0:T(8,128)}, u32[]{:S(2)}, u32[]{:S(2)}) %collective-permute-start) | collective-permute-done | bytes 1572896 | tf_op jit(solution)/shard_map/ppermute | solution.py:12
  114.1 2.7 constant_dynamic-update-slice_fusion.5
  116.8 2.7 constant_dynamic-update-slice_fusion.4
  120.7 2.7 constant_dynamic-update-slice_fusion.2
  123.5 22.6 %collective-permute-done.3 = f32[2,12,128,128]{3,2,1,0:T(8,128)S(1)} collective-permute-done((f32[2,12,128,128]{3,2,1,0:T(8,128)}, f32[2,12,128,128]{3,2,1,0:T(8,128)S(1)}, u32[]{:S(2)}, u32[]{:S(2)}) %collective-permute-start.3) | collective-permute-done | bytes 1572896 | tf_op jit(solution)/shard_map/ppermute | solution.py:12
  147.4 2.7 constant_dynamic-slice_fusion.1
  150.1 83.0 %while.10 = (s32[]{:T(128)}, f32[8,8,128,128]{3,2,1,0:T(8,128)}, s32[8]{0:T(128)S(1)}, pred[8,3,8]{2,1,0:T(4,128)(4,1)S(1)}, s32[8,3]{1,0:T(8,128)S(1)}, /*index...) while((s32[]{:T(128)}, f32[8,8,128,128]{3,2,1,0:T(8,128)}, ...), condition=%wide.region_3.4_spmd, body=%wide.region_2.3_spmd.sunk | while | flops 604373184 | bytes 10683783 | solution.py:50
  152.5 3.9 %gather_fusion = f32[24,128,128]{2,1,0:T(8,128)S(1)} fusion(f32[10,12,128,128]{3,2,1,0:T(8,128)} %get-tuple-element.151, s32[24]{0:T(128)S(1)} %reshape.83), kind=kCustom, calls=%fused_computation.clone.1 | custom fusion | bytes 3145920 | tf_op jit(solution)/shard_map/while/body/eval_jaxpr/gather | solution.py:45
  157.0 2.4 fusion.27
  162.8 3.9 %gather_fusion = f32[24,128,128]{2,1,0:T(8,128)S(1)} fusion(f32[10,12,128,128]{3,2,1,0:T(8,128)} %get-tuple-element.151, s32[24]{0:T(128)S(1)} %reshape.83), kind=kCustom, calls=%fused_computation.clone.1 | custom fusion | bytes 3145920 | tf_op jit(solution)/shard_map/while/body/eval_jaxpr/gather | solution.py:45
  167.3 2.4 fusion.27
  173.2 3.9 %gather_fusion = f32[24,128,128]{2,1,0:T(8,128)S(1)} fusion(f32[10,12,128,128]{3,2,1,0:T(8,128)} %get-tuple-element.151, s32[24]{0:T(128)S(1)} %reshape.83), kind=kCustom, calls=%fused_computation.clone.1 | custom fusion | bytes 3145920 | tf_op jit(solution)/shard_map/while/body/eval_jaxpr/gather | solution.py:45
  177.7 2.4 fusion.27
  183.6 3.9 %gather_fusion = f32[24,128,128]{2,1,0:T(8,128)S(1)} fusion(f32[10,12,128,128]{3,2,1,0:T(8,128)} %get-tuple-element.151, s32[24]{0:T(128)S(1)} %reshape.83), kind=kCustom, calls=%fused_computation.clone.1 | custom fusion | bytes 3145920 | tf_op jit(solution)/shard_map/while/body/eval_jaxpr/gather | solution.py:45
  188.1 2.4 fusion.27
  194.0 3.9 %gather_fusion = f32[24,128,128]{2,1,0:T(8,128)S(1)} fusion(f32[10,12,128,128]{3,2,1,0:T(8,128)} %get-tuple-element.151, s32[24]{0:T(128)S(1)} %reshape.83), kind=kCustom, calls=%fused_computation.clone.1 | custom fusion | bytes 3145920 | tf_op jit(solution)/shard_map/while/body/eval_jaxpr/gather | solution.py:45
  204.3 3.9 %gather_fusion = f32[24,128,128]{2,1,0:T(8,128)S(1)} fusion(f32[10,12,128,128]{3,2,1,0:T(8,128)} %get-tuple-element.151, s32[24]{0:T(128)S(1)} %reshape.83), kind=kCustom, calls=%fused_computation.clone.1 | custom fusion | bytes 3145920 | tf_op jit(solution)/shard_map/while/body/eval_jaxpr/gather | solution.py:45
  208.8 2.4 fusion.27
  214.7 3.9 %gather_fusion = f32[24,128,128]{2,1,0:T(8,128)S(1)} fusion(f32[10,12,128,128]{3,2,1,0:T(8,128)} %get-tuple-element.151, s32[24]{0:T(128)S(1)} %reshape.83), kind=kCustom, calls=%fused_computation.clone.1 | custom fusion | bytes 3145920 | tf_op jit(solution)/shard_map/while/body/eval_jaxpr/gather | solution.py:45
  225.1 3.9 %gather_fusion = f32[24,128,128]{2,1,0:T(8,128)S(1)} fusion(f32[10,12,128,128]{3,2,1,0:T(8,128)} %get-tuple-element.151, s32[24]{0:T(128)S(1)} %reshape.83), kind=kCustom, calls=%fused_computation.clone.1 | custom fusion | bytes 3145920 | tf_op jit(solution)/shard_map/while/body/eval_jaxpr/gather | solution.py:45
  233.1 114.7 %reduce-scatter.2.cloned.1.call-done = f32[2,8,128,128]{3,2,1,0:T(8,128)} async-done(((f32[8,8,128,128]{3,2,1,0:T(8,128)}), f32[2,8,128,128]{3,2,1,0:T(8,128)}) %reduce-scatter.2.cloned.1.call-update) | async-done | bytes 1048592 | tf_op jit(solution)/shard_map/reduce_scatter | solution.py:49
  (98 shorter events, 35.3 us)
Async XLA Ops:
  6.5 113.0 %copy-start = (f32[2,1,12,128,128]{4,3,2,1,0:T(8,128)S(1)}, f32[2,1,12,128,128]{4,3,2,1,0:T(8,128)}, u32[]{:S(2)}) copy-start(f32[2,1,12,128,128]{4,3,2,1,0:T(8,128)} %param.5) | copy-start | bytes 4718596
  6.5 140.8 %all-gather.2.cloned.1.call-start = ((), (), s32[]{:S(2)}) async-start(), calls=%async_computation.1 | async-start | bytes 7864320 | tf_op jit(solution)/shard_map/all_gather | solution.py:25
  7.3 340.5 %reduce-scatter.2.cloned.1.call-start = ((), (), s32[]{:S(2)}) async-start(), calls=%async_computation.2 | async-start | bytes 5242880 | tf_op jit(solution)/shard_map/reduce_scatter | solution.py:49
  7.3 106.8 %collective-permute-start = (f32[2,12,128,128]{3,2,1,0:T(8,128)}, f32[2,12,128,128]{3,2,1,0:T(8,128)}, u32[]{:S(2)}, u32[]{:S(2)}) collective-permute-start(f32[2,12,128,128]{3,2,1,0:T(8,128)} %bitcast.41), channel_id=1, source_target_pairs={{0,8},{4,12},{8,16},{12,20},{16,24},{20,28},{1,9},{5,13},{9,17},{1... | collective-permute-start | bytes 4718600 | tf_op jit(solution)/shard_map/ppermute | solution.py:12
  11.5 105.2 %collective-permute-start.1 = (f32[2,12,128,128]{3,2,1,0:T(8,128)}, f32[2,12,128,128]{3,2,1,0:T(8,128)}, u32[]{:S(2)}, u32[]{:S(2)}) collective-permute-start(f32[2,12,128,128]{3,2,1,0:T(8,128)} %bitcast.42), channel_id=1, source_target_pairs={{0,4},{4,8},{8,12},{12,16},{16,20},{20,24},{24,28},{1,5},{5,9},{9,... | collective-permute-start | bytes 4718600 | tf_op jit(solution)/shard_map/ppermute | solution.py:12
  14.7 106.0 %collective-permute-start.2 = (f32[2,12,128,128]{3,2,1,0:T(8,128)}, f32[2,12,128,128]{3,2,1,0:T(8,128)}, u32[]{:S(2)}, u32[]{:S(2)}) collective-permute-start(f32[2,12,128,128]{3,2,1,0:T(8,128)} %bitcast.43), channel_id=1, source_target_pairs={{4,0},{8,4},{12,8},{16,12},{20,16},{24,20},{28,24},{5,1},{9,5},{13... | collective-permute-start | bytes 4718600 | tf_op jit(solution)/shard_map/ppermute | solution.py:12
  19.5 126.6 %collective-permute-start.3 = (f32[2,12,128,128]{3,2,1,0:T(8,128)}, f32[2,12,128,128]{3,2,1,0:T(8,128)S(1)}, u32[]{:S(2)}, u32[]{:S(2)}) collective-permute-start(f32[2,12,128,128]{3,2,1,0:T(8,128)} %bitcast.44), channel_id=1, source_target_pairs={{8,0},{12,4},{16,8},{20,12},{24,16},{28,20},{9,1},{13,5},{17,9},{2... | collective-permute-start | bytes 4718600 | tf_op jit(solution)/shard_map/ppermute | solution.py:12
Sparse Core Ops, SparseCore 0:
  8.9 47.9 all-gather.1
  233.2 114.4 reduce-scatter.1
where the time goes:
time: 357 us; the launch traced here: 355 us
  waiting for transfers between devices  227 us (64%)
  local copies, waits for them, and re-layouts  64 us (18%)
  matrix products  19.4 us (5%)
  starting transfers between devices  14.2 us (4%)
  loops' own time  13.5 us (4%)
  between operations  13.5 us (4%)
    reduce_scatter x1, waiting for transfers between devices, on_device(): lax.psum_scatter(lax.map(one_row, jnp.arange(row_count * lax.axis_size('r...  115 us
    ppermute x4, waiting for transfers between devices, passed_along(): return lax.ppermute(x, axis, pairs)  111 us
    gather x16, local copies, waits for them, and re-layouts, one_row(): picked = window_rows[window_idx[row_index][:, None], slot_index[row_index]]  34.9 us
    dot_general x8, matrix products, one_row(): jnp.einsum('sab,sfbc->fac', entries[row_index], picked, precision=HIGHEST)  19.4 us
    ppermute x4, starting transfers between devices, passed_along(): return lax.ppermute(x, axis, pairs)  14.1 us
    another operation x1, loops' own time, on_device(): lax.map(one_row, jnp.arange(row_count * lax.axis_size('rep'), dtype=jnp.i...  13.5 us
    unnamed x7, local copies, waits for them, and re-layouts  10.2 us
    dynamic_update_slice x16, local copies, waits for them, and re-layouts, on_device(): lax.map(one_row, jnp.arange(row_count * lax.axis_size('rep'), dtype=jnp.i...  8.32 us
  transfers between devices with their start and end apart: 6, of which 3 were waited for; matrix products, arithmetic and copies ran while one was open for 4% of the time, Pallas kernels for 0%

commit v1 on v0

v1 whole, which is shorter than its diff:
```python
import jax
import jax.numpy as jnp
from jax import lax
from jax.experimental import pallas as pl
from jax.experimental.pallas import tpu as pltpu
from jax.sharding import PartitionSpec as P


def passed_along(x, axis, by):
    peers = lax.axis_size(axis)
    pairs = [(i, i + by) for i in range(peers) if 0 <= i + by < peers]
    return lax.ppermute(x, axis, pairs)


def two_part(x):
    high = x.astype(jnp.bfloat16)
    low = (x - high.astype(jnp.float32)).astype(jnp.bfloat16)
    return high, low


def products_kernel(table, entries_ref, window_ref, out_ref):
    row = pl.program_id(0)
    per_layer = entries_ref.shape[1]
    wanted = out_ref.shape[1]
    out_ref[...] = jnp.zeros_like(out_ref)
    for s in range(per_layer):
        a_high, a_low = two_part(entries_ref[0, s])

        def one_output(f, carry):
            where = table[(row * per_layer + s) * wanted + f]

            @pl.when(where >= 0)
            def _():
                b_high, b_low = two_part(window_ref[where])
                left = jnp.concatenate([a_high, a_low], axis=1)
                right = jnp.concatenate([b_high, b_high], axis=0)
                got = jnp.dot(left, right, preferred_element_type=jnp.float32)
                got += jnp.dot(a_high, b_low, preferred_element_type=jnp.float32)
                out_ref[0, f] += got

            return carry

        lax.fori_loop(0, wanted, one_output, 0, unroll=True)


def products(table, entries, window, wanted):
    rows, per_layer, order, _ = entries.shape
    return pl.pallas_call(
        products_kernel,
        out_shape=jax.ShapeDtypeStruct((rows, wanted, order, order), jnp.float32),
        grid_spec=pltpu.PrefetchScalarGridSpec(
            num_scalar_prefetch=1,
            grid=(rows,),
            in_specs=[
                pl.BlockSpec((1, per_layer, order, order), lambda r, t: (r, 0, 0, 0)),
                pl.BlockSpec(window.shape, lambda r, t: (0, 0, 0)),
            ],
            out_specs=pl.BlockSpec((1, wanted, order, order), lambda r, t: (r, 0, 0, 0)),
        ),
        compiler_params=pltpu.CompilerParams(vmem_limit_bytes=32 * 1024 * 1024),
        cost_estimate=pl.CostEstimate(
            flops=6 * rows * per_layer * wanted * order**3,
            bytes_accessed=4 * (window.size + entries.size + rows * wanted * order * order),
            transcendentals=0,
        ),
    )(table, entries, window)


def on_device(p_values, p_cols, out_cols):
    layers = lax.axis_size("rep")
    layer_index = lax.axis_index("rep")
    segment = lax.axis_index(("row", "col"))
    own_rows = p_values[:, 0]
    row_count, slot_total, order, _ = own_rows.shape
    per_layer = slot_total // layers
    seg_rows = row_count * layers
    wanted = out_cols.shape[1]
    ahead = passed_along(own_rows, ("row", "col"), 1)
    back = passed_along(own_rows, ("row", "col"), -1)
    ahead2 = passed_along(ahead, ("row", "col"), 1)
    back2 = passed_along(back, ("row", "col"), -1)
    gathered = lax.all_gather(p_values, "rep", axis=1, tiled=True)
    entries = lax.dynamic_slice_in_dim(gathered, layer_index * per_layer, per_layer, 2)
    entries = entries.reshape(seg_rows, per_layer, order, order)
    window = jnp.concatenate([ahead2, ahead, own_rows, back, back2], axis=0)
    window = window.reshape(-1, order, order)
    inner_cols = lax.dynamic_slice(
        p_cols, (segment * seg_rows, layer_index * per_layer), (seg_rows, per_layer)
    )
    far_cols = p_cols[inner_cols]
    slot_ids = jnp.arange(slot_total, dtype=jnp.int32)
    matches = far_cols[:, :, None, :] == out_cols[:, None, :, None]
    slot_index = jnp.max(jnp.where(matches, slot_ids, -1), axis=3)
    window_idx = inner_cols // layers - (segment - 2) * row_count
    table = jnp.where(slot_index >= 0, window_idx[:, :, None] * slot_total + slot_index, -1)
    shares = products(table.reshape(-1), entries, window, wanted)
    return lax.psum_scatter(shares, "rep", scatter_dimension=0, tiled=True)


def solution(mesh):
    in_specs = (P(("row", "col"), "rep", None, None, None), P(), P(("row", "col"), None))
    out_specs = P(("row", "col", "rep"), None, None, None)
    return jax.shard_map(
        on_device, mesh=mesh, in_specs=in_specs, out_specs=out_specs, check_vma=False
    )
```

time: 357 us -> 234 us (0.66)
  waiting for transfers between devices: 227 us -> 171 us
  local copies, waits for them, and re-layouts: 64 us -> 16.3 us
  matrix products: 19.4 us -> 0 us
  loops' own time: 13.5 us -> 0 us
  Pallas kernels: 0 us -> 10.7 us
    reduce_scatter x1, waiting for transfers between devices: 115 us -> 56.4 us  [on_device(): return lax.psum_scatter(shares, 'rep', scatter_dimension=0, tiled=True)]
    gather x16 -> x0, local copies, waits for them, and re-layouts: 34.9 us -> none  [one_row(): picked = window_rows[window_idx[row_index][:, None], slot_index[row_index]]]
    dot_general x8 -> x0, matrix products: 19.4 us -> none  [one_row(): jnp.einsum('sab,sfbc->fac', entries[row_index], picked, precision=HIGHEST)]
    another operation x1 -> x0, loops' own time: 13.5 us -> none  [on_device(): lax.map(one_row, jnp.arange(row_count * lax.axis_size('rep'), dtype=jnp.i...]
    pallas_call x0 -> x1, Pallas kernels: none -> 10.7 us  [products(): pl.pallas_call(products_kernel, out_shape=jax.ShapeDtypeStruct((rows, wan...]
    dynamic_update_slice x16 -> x0, local copies, waits for them, and re-layouts: 8.32 us -> none  [on_device(): lax.map(one_row, jnp.arange(row_count * lax.axis_size('rep'), dtype=jnp.i...]
    dynamic_slice x8 -> x0, local copies, waits for them, and re-layouts: 4.42 us -> none  [on_device(): lax.map(one_row, jnp.arange(row_count * lax.axis_size('rep'), dtype=jnp.i...]
    unnamed x7 -> x13, local copies, waits for them, and re-layouts: 10.2 us -> 12.3 us
  transfers between devices with their start and end apart: 6 -> 6, of which waited for: 3 -> 5; matrix products, arithmetic and copies ran while one was open for 4% -> 4% of each run, Pallas kernels for 0% -> 0%
where the time goes in v1:
time: 234 us; the launch traced here: 230 us
  waiting for transfers between devices  171 us (73%)
  starting transfers between devices  16.6 us (7%)
  local copies, waits for them, and re-layouts  16.3 us (7%)
  between operations  13.5 us (6%)
  Pallas kernels  10.7 us (5%)
    ppermute x4, waiting for transfers between devices, passed_along(): return lax.ppermute(x, axis, pairs)  114 us
    reduce_scatter x1, waiting for transfers between devices, on_device(): return lax.psum_scatter(shares, 'rep', scatter_dimension=0, tiled=True)  56.4 us
    ppermute x4, starting transfers between devices, passed_along(): return lax.ppermute(x, axis, pairs)  16.6 us
    unnamed x13, local copies, waits for them, and re-layouts  12.3 us
    pallas_call x1, Pallas kernels, products(): pl.pallas_call(products_kernel, out_shape=jax.ShapeDtypeStruct((rows, wan...  10.7 us
  transfers between devices with their start and end apart: 6, of which 5 were waited for; matrix products, arithmetic and copies ran while one was open for 4% of the time, Pallas kernels for 0%

profile of v1, /device:TPU:5, one launch (start us, length us, event | category | flops | bytes accessed | tf_op | source)
XLA Modules:
  0.0 230.3 jit_solution(4250490494023385277)
XLA Ops:
  6.5 0.7 all-gather.2.cloned.1.call-update
  7.3 3.2 %collective-permute-start = (f32[2,12,128,128]{3,2,1,0:T(8,128)}, f32[2,12,128,128]{3,2,1,0:T(8,128)}, u32[]{:S(2)}, u32[]{:S(2)}) collective-permute-start(f32[2,12,128,128]{3,2,1,0:T(8,128)} %bitcast.6), channel_id=1, source_target_pairs={{0,4},{4,8},{8,12},{12,16},{16,20},{20,24},{24,28},{1,5},{5,9},{9,... | collective-permute-start | bytes 4718600 | tf_op jit(solution)/shard_map/ppermute | solution.py:12
  10.5 4.8 %collective-permute-start.2 = (f32[2,12,128,128]{3,2,1,0:T(8,128)}, f32[2,12,128,128]{3,2,1,0:T(8,128)S(1)}, u32[]{:S(2)}, u32[]{:S(2)}) collective-permute-start(f32[2,12,128,128]{3,2,1,0:T(8,128)} %bitcast.7), channel_id=1, source_target_pairs={{4,0},{8,4},{12,8},{16,12},{20,16},{24,20},{28,24},{5,1},{9,5},{13... | collective-permute-start | bytes 4718600 | tf_op jit(solution)/shard_map/ppermute | solution.py:12
  15.3 32.2 %collective-permute-done = f32[2,12,128,128]{3,2,1,0:T(8,128)} collective-permute-done((f32[2,12,128,128]{3,2,1,0:T(8,128)}, f32[2,12,128,128]{3,2,1,0:T(8,128)}, u32[]{:S(2)}, u32[]{:S(2)}) %collective-permute-start) | collective-permute-done | bytes 1572896 | tf_op jit(solution)/shard_map/ppermute | solution.py:12
  47.5 1.9 collective-permute-start.1
  49.4 28.2 %collective-permute-done.2 = f32[2,12,128,128]{3,2,1,0:T(8,128)S(1)} collective-permute-done((f32[2,12,128,128]{3,2,1,0:T(8,128)}, f32[2,12,128,128]{3,2,1,0:T(8,128)S(1)}, u32[]{:S(2)}, u32[]{:S(2)}) %collective-permute-start.2) | collective-permute-done | bytes 1572896 | tf_op jit(solution)/shard_map/ppermute | solution.py:12
  77.6 6.7 %collective-permute-start.3 = (f32[2,12,128,128]{3,2,1,0:T(8,128)S(1)}, f32[2,12,128,128]{3,2,1,0:T(8,128)}, u32[]{:S(2)}, u32[]{:S(2)}) collective-permute-start(f32[2,12,128,128]{3,2,1,0:T(8,128)S(1)} %collective-permute-done.2), channel_id=1, source_target_pairs={{4,0},{8,4},{12,8},{16,12},{20,16},{24,20},{28,24},{5,1},{9,5},{13... | collective-permute-start | bytes 4718600 | tf_op jit(solution)/shard_map/ppermute | solution.py:12
  84.3 0.8 copy.11
  85.1 0.8 fusion.2
  86.1 0.6 gather_fusion
  86.7 1.2 select_reduce_fusion
  88.2 26.8 %collective-permute-done.1 = f32[2,12,128,128]{3,2,1,0:T(8,128)} collective-permute-done((f32[2,12,128,128]{3,2,1,0:T(8,128)}, f32[2,12,128,128]{3,2,1,0:T(8,128)}, u32[]{:S(2)}, u32[]{:S(2)}) %collective-permute-start.1) | collective-permute-done | bytes 1572896 | tf_op jit(solution)/shard_map/ppermute | solution.py:12
  115.0 1.5 constant_dynamic-update-slice_fusion.4
  116.5 1.5 constant_dynamic-update-slice_fusion.3
  118.0 0.1 constant_dynamic-update-slice_fusion.2
  118.1 0.2 constant_dynamic-update-slice_fusion.1
  118.3 26.6 %collective-permute-done.3 = f32[2,12,128,128]{3,2,1,0:T(8,128)} collective-permute-done((f32[2,12,128,128]{3,2,1,0:T(8,128)S(1)}, f32[2,12,128,128]{3,2,1,0:T(8,128)}, u32[]{:S(2)}, u32[]{:S(2)}) %collective-permute-start.3) | collective-permute-done | bytes 1572896 | tf_op jit(solution)/shard_map/ppermute | solution.py:12
  144.9 1.5 constant_dynamic-update-slice_fusion
  146.5 3.0 %copy-done.1 = f32[10,12,128,128]{3,2,1,0:T(8,128)} copy-done((f32[10,12,128,128]{3,2,1,0:T(8,128)}, f32[10,12,128,128]{3,2,1,0:T(8,128)S(1)}, u32[]{:S(2)}) %copy-start.1) | copy-done | bytes 7864344
  149.5 1.6 constant_dynamic-slice_fusion
  151.1 3.2 %copy-done.2 = f32[10,12,128,128]{3,2,1,0:T(8,128)S(1)} copy-done((f32[10,12,128,128]{3,2,1,0:T(8,128)S(1)}, f32[10,12,128,128]{3,2,1,0:T(8,128)}, u32[]{:S(2)}) %copy-start.2) | copy-done | bytes 7864344
  154.3 10.7 %shard_map.37 = f32[8,8,128,128]{3,2,1,0:T(8,128)S(1)} custom-call(s32[192]{0:T(256)S(1)} %select_n.33.table, f32[8,3,128,128]{3,2,1,0:T(8,128)S(1)} %bitcast.5, f32[120,128,128]{2,1,0:T(8,128)S(1)} %bitcast.4), custom_call_target="tpu_custom_call" | custom-call | flops 2415919104 | bytes 13631488 | tf_op jit(solution)/shard_map/pallas_call | solution.py:48
  165.1 1.9 copy-done
  167.0 56.4 %reduce-scatter.2.cloned.1.call-done = f32[2,8,128,128]{3,2,1,0:T(8,128)} async-done(((f32[8,8,128,128]{3,2,1,0:T(8,128)}), f32[2,8,128,128]{3,2,1,0:T(8,128)}) %reduce-scatter.2.cloned.1.call-update) | async-done | bytes 1048592 | tf_op jit(solution)/shard_map/reduce_scatter | solution.py:97
  (16 shorter events, 0.5 us)
Async XLA Ops:
  6.5 111.5 %copy-start.3 = (f32[2,1,12,128,128]{4,3,2,1,0:T(8,128)S(1)}, f32[2,1,12,128,128]{4,3,2,1,0:T(8,128)}, u32[]{:S(2)}) copy-start(f32[2,1,12,128,128]{4,3,2,1,0:T(8,128)} %param.3) | copy-start | bytes 4718596
  6.5 143.0 %all-gather.2.cloned.1.call-start = ((), (), s32[]{:S(2)}) async-start(), calls=%async_computation.1 | async-start | bytes 7864320 | tf_op jit(solution)/shard_map/all_gather | solution.py:82
  7.3 216.2 %reduce-scatter.2.cloned.1.call-start = ((), (), s32[]{:S(2)}) async-start(), calls=%async_computation.2 | async-start | bytes 5242880 | tf_op jit(solution)/shard_map/reduce_scatter | solution.py:97
  7.3 40.2 %collective-permute-start = (f32[2,12,128,128]{3,2,1,0:T(8,128)}, f32[2,12,128,128]{3,2,1,0:T(8,128)}, u32[]{:S(2)}, u32[]{:S(2)}) collective-permute-start(f32[2,12,128,128]{3,2,1,0:T(8,128)} %bitcast.6), channel_id=1, source_target_pairs={{0,4},{4,8},{8,12},{12,16},{16,20},{20,24},{24,28},{1,5},{5,9},{9,... | collective-permute-start | bytes 4718600 | tf_op jit(solution)/shard_map/ppermute | solution.py:12
  10.5 67.1 %collective-permute-start.2 = (f32[2,12,128,128]{3,2,1,0:T(8,128)}, f32[2,12,128,128]{3,2,1,0:T(8,128)S(1)}, u32[]{:S(2)}, u32[]{:S(2)}) collective-permute-start(f32[2,12,128,128]{3,2,1,0:T(8,128)} %bitcast.7), channel_id=1, source_target_pairs={{4,0},{8,4},{12,8},{16,12},{20,16},{24,20},{28,24},{5,1},{9,5},{13... | collective-permute-start | bytes 4718600 | tf_op jit(solution)/shard_map/ppermute | solution.py:12
  47.5 67.5 %collective-permute-start.1 = (f32[2,12,128,128]{3,2,1,0:T(8,128)}, f32[2,12,128,128]{3,2,1,0:T(8,128)}, u32[]{:S(2)}, u32[]{:S(2)}) collective-permute-start(f32[2,12,128,128]{3,2,1,0:T(8,128)} %collective-permute-done), channel_id=1, source_target_pairs={{0,4},{4,8},{8,12},{12,16},{16,20},{20,24},{24,28},{1,5},{5,9},{9,... | collective-permute-start | bytes 4718600 | tf_op jit(solution)/shard_map/ppermute | solution.py:12
  77.6 67.3 %collective-permute-start.3 = (f32[2,12,128,128]{3,2,1,0:T(8,128)S(1)}, f32[2,12,128,128]{3,2,1,0:T(8,128)}, u32[]{:S(2)}, u32[]{:S(2)}) collective-permute-start(f32[2,12,128,128]{3,2,1,0:T(8,128)S(1)} %collective-permute-done.2), channel_id=1, source_target_pairs={{4,0},{8,4},{12,8},{16,12},{20,16},{24,20},{28,24},{5,1},{9,5},{13... | collective-permute-start | bytes 4718600 | tf_op jit(solution)/shard_map/ppermute | solution.py:12
  146.5 3.1 %copy-start.1 = (f32[10,12,128,128]{3,2,1,0:T(8,128)}, f32[10,12,128,128]{3,2,1,0:T(8,128)S(1)}, u32[]{:S(2)}) copy-start(f32[10,12,128,128]{3,2,1,0:T(8,128)S(1)} %constant_dynamic-update-slice_fusion) | copy-start | bytes 23592964
  151.1 3.2 %copy-start.2 = (f32[10,12,128,128]{3,2,1,0:T(8,128)S(1)}, f32[10,12,128,128]{3,2,1,0:T(8,128)}, u32[]{:S(2)}) copy-start(f32[10,12,128,128]{3,2,1,0:T(8,128)} %copy-done.1) | copy-start | bytes 23592964
  165.0 1.9 copy-start
Sparse Core Ops, SparseCore 0:
  8.9 47.9 all-gather.1
  167.1 56.2 reduce-scatter.1

commit v2 on v1

--- a/solution.py
+++ b/solution.py
@@ -1,3 +1,5 @@
+import functools
+
 import jax
 import jax.numpy as jnp
 from jax import lax
@@ -6,10 +8,173 @@
 from jax.sharding import PartitionSpec as P
 
 
-def passed_along(x, axis, by):
-    peers = lax.axis_size(axis)
-    pairs = [(i, i + by) for i in range(peers) if 0 <= i + by < peers]
-    return lax.ppermute(x, axis, pairs)
+CHUNKS = 4
+MESH = pl.DeviceIdType.MESH
+
+
+def window_kernel(
+    rows, cols, own, win, transit, kept_sem, own_send, relay_send, transit_send, win_recv, transit_recv
+):
+    r, c = lax.axis_index("row"), lax.axis_index("col")
+    last = cols - 1
+    segment = r * cols + c
+    size = own.shape[0] // CHUNKS
+    at_edge = (c == 0) | (c == last)
+
+    barrier = pltpu.get_barrier_semaphore()
+
+    def greet(to_row, to_col):
+        pl.semaphore_signal(
+            barrier, inc=1, device_id={"row": to_row, "col": to_col}, device_id_type=MESH
+        )
+
+    greet(r, lax.rem(c + 1, cols))
+    greet(r, lax.rem(c + cols - 1, cols))
+    pl.when(at_edge & (r > 0))(lambda: greet(r - 1, c))
+    pl.when(at_edge & (r < rows - 1))(lambda: greet(r + 1, c))
+    peers = 2 + jnp.where(at_edge & (r > 0), 1, 0) + jnp.where(at_edge & (r < rows - 1), 1, 0)
+    pl.semaphore_wait(barrier, peers)
+
+    def part(k):
+        return pl.ds(k * size, size)
+
+    def slot(d, p):
+        return (1 - p) if d == 0 else (3 + p)
+
+    def step(d):
+        return 1 if d == 0 else -1
+
+    def in_range(at):
+        return (at >= 0) & (at < rows * cols)
+
+    def copy(source, target, sent, landed, to_row, to_col):
+        return pltpu.make_async_remote_copy(
+            src_ref=source,
+            dst_ref=target,
+            send_sem=sent,
+            recv_sem=landed,
+            device_id={"row": to_row, "col": to_col},
+            device_id_type=MESH,
+        )
+
+    def outgoing(d, p, k):
+        by = step(d)
+        leaves = c == (last if d == 0 else 0)
+        sends = in_range(segment + by)
+        if p == 1:
+            sends = sends & in_range(segment - by)
+        source = own.at[part(k)] if p == 0 else win.at[slot(d, 0), part(k)]
+        sent = own_send.at[d, k] if p == 0 else relay_send.at[d, k]
+        near = copy(
+            source, win.at[slot(d, p), part(k)], sent, win_recv.at[d, p, k], r, c + by
+        )
+        if k % 2 == 0:
+            place = (r + by, c)
+        else:
+            place = (r, 0 if d == 0 else last)
+        far = copy(
+            source, transit.at[d, p, part(k)], sent, transit_recv.at[d, p, k], *place
+        )
+        return near, sends & jnp.logical_not(leaves), far, sends & leaves
+
+    def passing(d, p, k):
+        by = step(d)
+        if k % 2 == 0:
+            mine = (c == last) & (r > 0) if d == 0 else (c == 0) & (r < rows - 1)
+            place = (r, 0 if d == 0 else last)
+        else:
+            mine = (c == 0) & (r < rows - 1) if d == 0 else (c == last) & (r > 0)
+            place = (r + by, c)
+        onward = copy(
+            transit.at[d, p, part(k)],
+            win.at[slot(d, p), part(k)],
+            transit_send.at[d, p, k],
+            win_recv.at[d, p, k],
+            *place,
+        )
+        return onward, mine
+
+    def landing(d, p, k):
+        target = win.at[slot(d, p), part(k)]
+        arrives = in_range(segment - (1 + p) * step(d))
+        done = copy(target, target, own_send.at[d, k], win_recv.at[d, p, k], r, lax.rem(c + 1, cols))
+        return done, arrives
+
+    def send(d, p, k):
+        near, near_on, far, far_on = outgoing(d, p, k)
+        pl.when(near_on)(near.start)
+        pl.when(far_on)(far.start)
+
+    def pass_on(d, p, k):
+        onward, mine = passing(d, p, k)
+
+        @pl.when(mine)
+        def _():
+            held = transit.at[d, p, part(k)]
+            copy(
+                held, held, own_send.at[d, k], transit_recv.at[d, p, k], r, lax.rem(c + 1, cols)
+            ).wait_recv()
+            onward.start()
+
+    def land(d, p, k):
+        done, arrives = landing(d, p, k)
+        pl.when(arrives)(done.wait_recv)
+
+    for k in (1, 0, 3, 2):
+        for d in range(2):
+            send(d, 0, k)
+    kept = pltpu.make_async_copy(own, win.at[2], kept_sem)
+    kept.start()
+    order = (1, 0, 3, 2)
+    for i in range(CHUNKS + 1):
+        if i < CHUNKS:
+            for d in range(2):
+                pass_on(d, 0, order[i])
+            for d in range(2):
+                land(d, 0, order[i])
+                send(d, 1, order[i])
+        if i > 0:
+            for d in range(2):
+                pass_on(d, 1, order[i - 1])
+    for k in order:
+        for d in range(2):
+            land(d, 1, k)
+    kept.wait()
+    for k in range(CHUNKS):
+        for d in range(2):
+            for p in range(2):
+                near, near_on, far, far_on = outgoing(d, p, k)
+                pl.when(near_on)(near.wait_send)
+                pl.when(far_on)(far.wait_send)
+                onward, mine = passing(d, p, k)
+                pl.when(mine)(onward.wait_send)
+
+
+def gathered_window(own):
+    rows, cols = lax.axis_size("row"), lax.axis_size("col")
+    blocks, order, _ = own.shape
+    dma = pltpu.SemaphoreType.DMA
+    return pl.pallas_call(
+        functools.partial(window_kernel, rows, cols),
+        out_shape=jax.ShapeDtypeStruct((5, blocks, order, order), own.dtype),
+        in_specs=[pl.BlockSpec(memory_space=pl.ANY)],
+        out_specs=pl.BlockSpec(memory_space=pl.ANY),
+        scratch_shapes=[
+            pltpu.VMEM((2, 2, blocks, order, order), own.dtype),
+            dma,
+            dma((2, CHUNKS)),
+            dma((2, CHUNKS)),
+            dma((2, 2, CHUNKS)),
+            dma((2, 2, CHUNKS)),
+            dma((2, 2, CHUNKS)),
+        ],
+        compiler_params=pltpu.CompilerParams(
+            collective_id=0, has_side_effects=True, vmem_limit_bytes=32 * 1024 * 1024
+        ),
+        cost_estimate=pl.CostEstimate(
+            flops=0, bytes_accessed=16 * own.size * 5, transcendentals=0
+        ),
+    )(own)
 
 
 def two_part(x):
@@ -75,14 +240,10 @@
     per_layer = slot_total // layers
     seg_rows = row_count * layers
     wanted = out_cols.shape[1]
-    ahead = passed_along(own_rows, ("row", "col"), 1)
-    back = passed_along(own_rows, ("row", "col"), -1)
-    ahead2 = passed_along(ahead, ("row", "col"), 1)
-    back2 = passed_along(back, ("row", "col"), -1)
     gathered = lax.all_gather(p_values, "rep", axis=1, tiled=True)
     entries = lax.dynamic_slice_in_dim(gathered, layer_index * per_layer, per_layer, 2)
     entries = entries.reshape(seg_rows, per_layer, order, order)
-    window = jnp.concatenate([ahead2, ahead, own_rows, back, back2], axis=0)
+    window = gathered_window(own_rows.reshape(-1, order, order))
     window = window.reshape(-1, order, order)
     inner_cols = lax.dynamic_slice(
         p_cols, (segment * seg_rows, layer_index * per_layer), (seg_rows, per_layer)

time: 234 us -> 202 us (0.86); the launches traced: 230 us -> 201 us
  waiting for transfers between devices: 171 us -> 58.5 us
  Pallas kernels: 10.7 us -> 114 us
  starting transfers between devices: 16.6 us -> 0.04 us
  local copies, waits for them, and re-layouts: 16.3 us -> 12.9 us
    ppermute x4 -> x0, waiting for transfers between devices: 114 us -> none  [passed_along(): return lax.ppermute(x, axis, pairs)]
    pallas_call x0 -> x1, Pallas kernels: none -> 103 us  [gathered_window(): pl.pallas_call(functools.partial(window_kernel, rows, cols), out_shape=ja...]
    ppermute x4 -> x0, starting transfers between devices: 16.6 us -> none  [passed_along(): return lax.ppermute(x, axis, pairs)]
    unnamed x13 -> x9, local copies, waits for them, and re-layouts: 12.3 us -> 10.4 us
  transfers between devices with their start and end apart: 6 -> 2, of which waited for: 5 -> 1; matrix products, arithmetic and copies ran while one was open for 4% -> 2% of each run, Pallas kernels for 0% -> 51%
where the time goes in v2:
time: 202 us; the launch traced here: 201 us
  Pallas kernels  114 us (56%)
  waiting for transfers between devices  58.5 us (29%)
  between operations  13.5 us (7%)
  local copies, waits for them, and re-layouts  12.9 us (6%)
  other arithmetic  2.1 us (1%)
    pallas_call x1, Pallas kernels, gathered_window(): pl.pallas_call(functools.partial(window_kernel, rows, cols), out_shape=ja...  103 us
    reduce_scatter x1, waiting for transfers between devices, on_device(): return lax.psum_scatter(shares, 'rep', scatter_dimension=0, tiled=True)  57.8 us
    pallas_call x1, Pallas kernels, products(): pl.pallas_call(products_kernel, out_shape=jax.ShapeDtypeStruct((rows, wan...  11.1 us
    unnamed x9, local copies, waits for them, and re-layouts  10.4 us
  transfers between devices with their start and end apart: 2, of which 1 were waited for; matrix products, arithmetic and copies ran while one was open for 2% of the time, Pallas kernels for 51%

profile of v2, /device:TPU:5, one launch (start us, length us, event | category | flops | bytes accessed | tf_op | source)
XLA Modules:
  0.0 201.1 jit_solution(816454885594432541)
XLA Ops:
  6.5 0.0 all-gather.2.cloned.1.call-start
  6.5 0.7 all-gather.2.cloned.1.call-update
  7.3 0.0 reduce-scatter.2.cloned.1.call-start
  7.3 0.8 copy.11
  8.1 0.8 fusion.2
  8.9 0.1 copy.12
  9.0 0.1 copy.10
  9.0 0.1 reshape.22
  9.1 0.6 gather_fusion
  9.7 1.2 select_reduce_fusion
  11.0 0.1 add_select_fusion
  11.0 0.1 select_n.33.table
  11.1 0.0 copy-start.3
  11.1 1.4 copy-done.3
  12.5 103.0 %shard_map.37 = f32[5,24,128,128]{3,2,1,0:T(8,128)S(1)} custom-call(f32[24,128,128]{2,1,0:T(8,128)S(1)} %bitcast.4), custom_call_target="tpu_custom_call" | custom-call | bytes 31457280 | tf_op jit(solution)/shard_map/pallas_call | solution.py:157
  115.5 0.0 copy-start
  115.6 3.1 %copy-done = f32[5,24,128,128]{3,2,1,0:T(8,128)} copy-done((f32[5,24,128,128]{3,2,1,0:T(8,128)}, f32[5,24,128,128]{3,2,1,0:T(8,128)S(1)}, u32[]{:S(2)}) %copy-start) | copy-done | bytes 7864344
  118.6 1.6 constant_dynamic-slice_fusion
  120.2 0.0 copy-start.1
  120.2 3.2 %copy-done.1 = f32[5,24,128,128]{3,2,1,0:T(8,128)S(1)} copy-done((f32[5,24,128,128]{3,2,1,0:T(8,128)S(1)}, f32[5,24,128,128]{3,2,1,0:T(8,128)}, u32[]{:S(2)}) %copy-start.1) | copy-done | bytes 7864344
  123.4 11.1 %shard_map.38 = f32[8,8,128,128]{3,2,1,0:T(8,128)S(1)} custom-call(s32[192]{0:T(256)S(1)} %select_n.33.table, f32[8,3,128,128]{3,2,1,0:T(8,128)S(1)} %bitcast.5, f32[120,128,128]{2,1,0:T(8,128)S(1)} %bitcast.3), custom_call_target="tpu_custom_call" | custom-call | flops 2415919104 | bytes 13631488 | tf_op jit(solution)/shard_map/pallas_call | solution.py:213
  134.5 1.9 copy-done.2
  136.4 0.0 reduce-scatter.2.cloned.1.call-update
  136.4 57.8 %reduce-scatter.2.cloned.1.call-done = f32[2,8,128,128]{3,2,1,0:T(8,128)} async-done(((f32[8,8,128,128]{3,2,1,0:T(8,128)}), f32[2,8,128,128]{3,2,1,0:T(8,128)}) %reduce-scatter.2.cloned.1.call-update) | async-done | bytes 1048592 | tf_op jit(solution)/shard_map/reduce_scatter | solution.py:258
  (4 shorter events, 0.0 us)
Async XLA Ops:
  6.5 112.1 %all-gather.2.cloned.1.call-start = ((), (), s32[]{:S(2)}) async-start(), calls=%async_computation.1 | async-start | bytes 7864320 | tf_op jit(solution)/shard_map/all_gather | solution.py:243
  7.3 187.0 %reduce-scatter.2.cloned.1.call-start = ((), (), s32[]{:S(2)}) async-start(), calls=%async_computation.2 | async-start | bytes 5242880 | tf_op jit(solution)/shard_map/reduce_scatter | solution.py:258
  11.1 1.4 copy-start.3
  115.5 3.1 %copy-start = (f32[5,24,128,128]{3,2,1,0:T(8,128)}, f32[5,24,128,128]{3,2,1,0:T(8,128)S(1)}, u32[]{:S(2)}) copy-start(f32[5,24,128,128]{3,2,1,0:T(8,128)S(1)} %shard_map.37) | copy-start | bytes 23592964
  120.2 3.2 %copy-start.1 = (f32[5,24,128,128]{3,2,1,0:T(8,128)S(1)}, f32[5,24,128,128]{3,2,1,0:T(8,128)}, u32[]{:S(2)}) copy-start(f32[5,24,128,128]{3,2,1,0:T(8,128)} %copy-done) | copy-start | bytes 23592964
  134.5 1.9 copy-start.2
Sparse Core Ops, SparseCore 0:
  8.9 47.9 all-gather.1
  136.6 57.6 reduce-scatter.1

commit v3 on v2

--- a/solution.py
+++ b/solution.py
@@ -231,6 +231,94 @@
     )(table, entries, window)
 
 
+PIECES = 2
+
+
+def share_sum_kernel(shares, out, from_twin, to_far, from_far, twin_send, twin_recv, far_send, far_recv):
+    me = lax.axis_index("rep")
+    twin = me + 1 - 2 * lax.rem(me, 2)
+    far = lax.rem(me + 2, 4)
+    far_twin = lax.rem(twin + 2, 4)
+    rows = out.shape[0]
+    size = out.shape[1] // PIECES
+
+    barrier = pltpu.get_barrier_semaphore()
+    for peer in (twin, far):
+        pl.semaphore_signal(barrier, inc=1, device_id={"rep": peer}, device_id_type=MESH)
+    pl.semaphore_wait(barrier, 2)
+
+    pieces = [(q, i) for q in range(rows) for i in range(PIECES)]
+
+    def twin_copy(h, q, i):
+        owner = far_twin if h == 0 else twin
+        return pltpu.make_async_remote_copy(
+            src_ref=shares.at[owner * rows + q, pl.ds(i * size, size)],
+            dst_ref=from_twin.at[h, q, pl.ds(i * size, size)],
+            send_sem=twin_send.at[h, q, i],
+            recv_sem=twin_recv.at[h, q, i],
+            device_id={"rep": twin},
+            device_id_type=MESH,
+        )
+
+    def far_copy(q, i):
+        return pltpu.make_async_remote_copy(
+            src_ref=to_far.at[q, pl.ds(i * size, size)],
+            dst_ref=from_far.at[q, pl.ds(i * size, size)],
+            send_sem=far_send.at[q, i],
+            recv_sem=far_recv.at[q, i],
+            device_id={"rep": far},
+            device_id_type=MESH,
+        )
+
+    for h in range(2):
+        for q, i in pieces:
+            twin_copy(h, q, i).start()
+    for q, i in pieces:
+        part = pl.ds(i * size, size)
+        twin_copy(0, q, i).wait_recv()
+        to_far[q, part] = shares[far * rows + q, part] + from_twin[0, q, part]
+        far_copy(q, i).start()
+    for q, i in pieces:
+        part = pl.ds(i * size, size)
+        twin_copy(1, q, i).wait_recv()
+        out[q, part] = shares[me * rows + q, part] + from_twin[1, q, part]
+    for q, i in pieces:
+        part = pl.ds(i * size, size)
+        far_copy(q, i).wait_recv()
+        out[q, part] = out[q, part] + from_far[q, part]
+    for q, i in pieces:
+        far_copy(q, i).wait_send()
+        for h in range(2):
+            twin_copy(h, q, i).wait_send()
+
+
+def summed_shares(shares):
+    assert lax.axis_size("rep") == 4
+    kept = (shares.shape[0] // 4,) + shares.shape[1:]
+    dma = pltpu.SemaphoreType.DMA
+    return pl.pallas_call(
+        share_sum_kernel,
+        out_shape=jax.ShapeDtypeStruct(kept, shares.dtype),
+        in_specs=[pl.BlockSpec(memory_space=pltpu.VMEM)],
+        out_specs=pl.BlockSpec(memory_space=pltpu.VMEM),
+        scratch_shapes=[
+            pltpu.VMEM((2,) + kept, shares.dtype),
+            pltpu.VMEM(kept, shares.dtype),
+            pltpu.VMEM(kept, shares.dtype),
+            dma((2, kept[0], PIECES)),
+            dma((2, kept[0], PIECES)),
+            dma((kept[0], PIECES)),
+            dma((kept[0], PIECES)),
+        ],
+        compiler_params=pltpu.CompilerParams(
+            collective_id=1, has_side_effects=True, vmem_limit_bytes=32 * 1024 * 1024
+        ),
+        cost_estimate=pl.CostEstimate(
+            flops=shares.size, bytes_accessed=8 * shares.size, transcendentals=0
+        ),
+    )(shares)
+
+
 def on_device(p_values, p_cols, out_cols):
     layers = lax.axis_size("rep")
     layer_index = lax.axis_index("rep")
@@ -255,7 +343,7 @@
     window_idx = inner_cols // layers - (segment - 2) * row_count
     table = jnp.where(slot_index >= 0, window_idx[:, :, None] * slot_total + slot_index, -1)
     shares = products(table.reshape(-1), entries, window, wanted)
-    return lax.psum_scatter(shares, "rep", scatter_dimension=0, tiled=True)
+    return summed_shares(shares)
 
 
 def solution(mesh):

time: 202 us -> 182 us (0.901)
  the two profiles are of different devices: /device:TPU:5 before, /device:TPU:0 now
where the time goes in v3:
time: 182 us; the launch traced here: 181 us
  Pallas kernels  153 us (84%)
  between operations  13.5 us (7%)
  local copies, waits for them, and re-layouts  11.9 us (7%)
  other arithmetic  2.1 us (1%)
    pallas_call x1, Pallas kernels, gathered_window(): pl.pallas_call(functools.partial(window_kernel, rows, cols), out_shape=ja...  107 us
    pallas_call x1, Pallas kernels, summed_shares(): pl.pallas_call(share_sum_kernel, out_shape=jax.ShapeDtypeStruct(kept, sha...  25.6 us
    pallas_call x1, Pallas kernels, products(): pl.pallas_call(products_kernel, out_shape=jax.ShapeDtypeStruct((rows, wan...  20.2 us
    unnamed x8, local copies, waits for them, and re-layouts  9.45 us
  transfers between devices with their start and end apart: 1, of which 0 were waited for; matrix products, arithmetic and copies ran while one was open for 2% of the time, Pallas kernels for 59%

profile of v3, /device:TPU:0, one launch (start us, length us, event | category | flops | bytes accessed | tf_op | source)
XLA Modules:
  0.0 181.4 jit_solution(3924717311231401327)
XLA Ops:
  6.5 0.0 all-gather.2.cloned.1.call-start
  6.5 0.7 all-gather.2.cloned.1.call-update
  7.3 0.8 copy.11
  8.1 0.8 fusion.2
  8.8 0.1 copy.12
  8.9 0.1 copy.10
  9.0 0.1 reshape.22
  9.1 0.6 gather_fusion
  9.7 1.2 select_reduce_fusion
  10.9 0.1 add_select_fusion
  11.0 0.1 select_n.33.table
  11.1 0.0 copy-start.2
  11.1 1.4 copy-done.2
  12.5 107.4 %shard_map.37 = f32[5,24,128,128]{3,2,1,0:T(8,128)S(1)} custom-call(f32[24,128,128]{2,1,0:T(8,128)S(1)} %bitcast.4), custom_call_target="tpu_custom_call" | custom-call | bytes 31457280 | tf_op jit(solution)/shard_map/pallas_call | solution.py:157
  119.9 0.0 copy-start
  119.9 3.1 %copy-done = f32[5,24,128,128]{3,2,1,0:T(8,128)} copy-done((f32[5,24,128,128]{3,2,1,0:T(8,128)}, f32[5,24,128,128]{3,2,1,0:T(8,128)S(1)}, u32[]{:S(2)}) %copy-start) | copy-done | bytes 7864344
  123.0 0.0 all-gather.2.cloned.1.call-done
  123.0 1.6 constant_dynamic-slice_fusion
  124.6 0.0 copy-start.1
  124.6 3.2 %copy-done.1 = f32[5,24,128,128]{3,2,1,0:T(8,128)S(1)} copy-done((f32[5,24,128,128]{3,2,1,0:T(8,128)S(1)}, f32[5,24,128,128]{3,2,1,0:T(8,128)}, u32[]{:S(2)}) %copy-start.1) | copy-done | bytes 7864344
  127.8 20.2 %shard_map.38.shares = f32[8,8,128,128]{3,2,1,0:T(8,128)S(1)} custom-call(s32[192]{0:T(256)S(1)} %select_n.33.table, f32[8,3,128,128]{3,2,1,0:T(8,128)S(1)} %bitcast.5, f32[120,128,128]{2,1,0:T(8,128)S(1)} %bitcast.3), custom_call_target="tpu_custom_call" | custom-call | flops 2415919104 | bytes 13631488 | tf_op jit(solution)/shard_map/pallas_call | solution.py:213
  148.0 25.6 %shard_map.39 = f32[2,8,128,128]{3,2,1,0:T(8,128)S(1)} custom-call(f32[8,8,128,128]{3,2,1,0:T(8,128)S(1)} %shard_map.38.shares), custom_call_target="tpu_custom_call" | custom-call | flops 1048576 | bytes 8388608 | tf_op jit(solution)/shard_map/pallas_call | solution.py:299
  173.6 1.0 copy.14
  (2 shorter events, 0.0 us)
Async XLA Ops:
  6.5 116.5 %all-gather.2.cloned.1.call-start = ((), (), s32[]{:S(2)}) async-start(), calls=%async_computation | async-start | bytes 7864320 | tf_op jit(solution)/shard_map/all_gather | solution.py:331
  11.1 1.4 copy-start.2
  119.9 3.1 %copy-start = (f32[5,24,128,128]{3,2,1,0:T(8,128)}, f32[5,24,128,128]{3,2,1,0:T(8,128)S(1)}, u32[]{:S(2)}) copy-start(f32[5,24,128,128]{3,2,1,0:T(8,128)S(1)} %shard_map.37) | copy-start | bytes 23592964
  124.6 3.2 %copy-start.1 = (f32[5,24,128,128]{3,2,1,0:T(8,128)S(1)}, f32[5,24,128,128]{3,2,1,0:T(8,128)}, u32[]{:S(2)}) copy-start(f32[5,24,128,128]{3,2,1,0:T(8,128)} %copy-done) | copy-start | bytes 23592964
Sparse Core Ops, SparseCore 0:
  8.9 49.0 all-gather.1

commit v4 on v3

--- a/solution.py
+++ b/solution.py
@@ -186,26 +186,29 @@
 def products_kernel(table, entries_ref, window_ref, out_ref):
     row = pl.program_id(0)
     per_layer = entries_ref.shape[1]
-    wanted = out_ref.shape[1]
-    out_ref[...] = jnp.zeros_like(out_ref)
+    wanted, order = out_ref.shape[1], out_ref.shape[3]
+    left = []
     for s in range(per_layer):
         a_high, a_low = two_part(entries_ref[0, s])
-
-        def one_output(f, carry):
-            where = table[(row * per_layer + s) * wanted + f]
-
-            @pl.when(where >= 0)
-            def _():
-                b_high, b_low = two_part(window_ref[where])
-                left = jnp.concatenate([a_high, a_low], axis=1)
-                right = jnp.concatenate([b_high, b_high], axis=0)
-                got = jnp.dot(left, right, preferred_element_type=jnp.float32)
-                got += jnp.dot(a_high, b_low, preferred_element_type=jnp.float32)
-                out_ref[0, f] += got
-
-            return carry
-
-        lax.fori_loop(0, wanted, one_output, 0, unroll=True)
+        left += [a_high, a_low, a_high]
+    left = jnp.concatenate(left, axis=1)
+    group = 2 if wanted % 2 == 0 else 1
+    for first in range(0, wanted, group):
+        columns = []
+        for f in range(first, first + group):
+            right = []
+            for s in range(per_layer):
+                where = table[(row * per_layer + s) * wanted + f]
+                block = window_ref[jnp.maximum(where, 0)]
+                block = jnp.where(where >= 0, block, jnp.zeros_like(block))
+                b_high, b_low = two_part(block)
+                right += [b_high, b_high, b_low]
+            columns.append(jnp.concatenate(right, axis=0))
+        got = jnp.dot(
+            left, jnp.concatenate(columns, axis=1), preferred_element_type=jnp.float32
+        )
+        for at in range(group):
+            out_ref[0, first + at] = got[:, at * order : (at + 1) * order]
 
 
 def products(table, entries, window, wanted):

time: 182 us -> 171 us (0.940)
  the two profiles are of different devices: /device:TPU:0 before, /device:TPU:5 now
where the time goes in v4:
time: 171 us
  Pallas kernels  143 us (84%)
  between operations  13.5 us (8%)
  local copies, waits for them, and re-layouts  11.9 us (7%)
  other arithmetic  2.1 us (1%)
    pallas_call x1, Pallas kernels, gathered_window(): pl.pallas_call(functools.partial(window_kernel, rows, cols), out_shape=ja...  103 us
    pallas_call x1, Pallas kernels, summed_shares(): pl.pallas_call(share_sum_kernel, out_shape=jax.ShapeDtypeStruct(kept, sha...  34.9 us
    unnamed x8, local copies, waits for them, and re-layouts  9.45 us
    pallas_call x1, Pallas kernels, products(): pl.pallas_call(products_kernel, out_shape=jax.ShapeDtypeStruct((rows, wan...  4.96 us
  transfers between devices with their start and end apart: 1, of which 0 were waited for; matrix products, arithmetic and copies ran while one was open for 2% of the time, Pallas kernels for 60%

profile of v4, /device:TPU:5, one launch (start us, length us, event | category | flops | bytes accessed | tf_op | source)
XLA Modules:
  0.0 171.1 jit_solution(1986270074136208420)
XLA Ops:
  6.5 0.0 all-gather.2.cloned.1.call-start
  6.5 0.7 all-gather.2.cloned.1.call-update
  7.3 0.8 copy.11
  8.1 0.8 fusion.2
  8.8 0.1 copy.12
  8.9 0.1 copy.10
  9.0 0.1 reshape.22
  9.1 0.6 gather_fusion
  9.7 1.2 select_reduce_fusion
  10.9 0.1 add_select_fusion
  11.0 0.1 select_n.33.table
  11.1 0.0 copy-start.2
  11.1 1.4 copy-done.2
  12.5 103.0 %shard_map.37 = f32[5,24,128,128]{3,2,1,0:T(8,128)S(1)} custom-call(f32[24,128,128]{2,1,0:T(8,128)S(1)} %bitcast.4), custom_call_target="tpu_custom_call" | custom-call | bytes 31457280 | tf_op jit(solution)/shard_map/pallas_call | solution.py:157
  115.5 0.0 copy-start
  115.5 3.1 %copy-done = f32[5,24,128,128]{3,2,1,0:T(8,128)} copy-done((f32[5,24,128,128]{3,2,1,0:T(8,128)}, f32[5,24,128,128]{3,2,1,0:T(8,128)S(1)}, u32[]{:S(2)}) %copy-start) | copy-done | bytes 7864344
  118.6 0.0 all-gather.2.cloned.1.call-done
  118.6 1.6 constant_dynamic-slice_fusion
  120.1 0.0 copy-start.1
  120.1 3.2 %copy-done.1 = f32[5,24,128,128]{3,2,1,0:T(8,128)S(1)} copy-done((f32[5,24,128,128]{3,2,1,0:T(8,128)S(1)}, f32[5,24,128,128]{3,2,1,0:T(8,128)}, u32[]{:S(2)}) %copy-start.1) | copy-done | bytes 7864344
  123.4 5.0 %shard_map.38.shares = f32[8,8,128,128]{3,2,1,0:T(8,128)S(1)} custom-call(s32[192]{0:T(256)S(1)} %select_n.33.table, f32[8,3,128,128]{3,2,1,0:T(8,128)S(1)} %bitcast.5, f32[120,128,128]{2,1,0:T(8,128)S(1)} %bitcast.3), custom_call_target="tpu_custom_call" | custom-call | flops 2415919104 | bytes 13631488 | tf_op jit(solution)/shard_map/pallas_call | solution.py:216
  128.3 34.9 %shard_map.39 = f32[2,8,128,128]{3,2,1,0:T(8,128)S(1)} custom-call(f32[8,8,128,128]{3,2,1,0:T(8,128)S(1)} %shard_map.38.shares), custom_call_target="tpu_custom_call" | custom-call | flops 1048576 | bytes 8388608 | tf_op jit(solution)/shard_map/pallas_call | solution.py:302
  163.3 1.0 copy.14
  (2 shorter events, 0.0 us)
Async XLA Ops:
  6.5 112.0 %all-gather.2.cloned.1.call-start = ((), (), s32[]{:S(2)}) async-start(), calls=%async_computation | async-start | bytes 7864320 | tf_op jit(solution)/shard_map/all_gather | solution.py:334
  11.1 1.4 copy-start.2
  115.5 3.1 %copy-start = (f32[5,24,128,128]{3,2,1,0:T(8,128)}, f32[5,24,128,128]{3,2,1,0:T(8,128)S(1)}, u32[]{:S(2)}) copy-start(f32[5,24,128,128]{3,2,1,0:T(8,128)S(1)} %shard_map.37) | copy-start | bytes 23592964
  120.1 3.2 %copy-start.1 = (f32[5,24,128,128]{3,2,1,0:T(8,128)S(1)}, f32[5,24,128,128]{3,2,1,0:T(8,128)}, u32[]{:S(2)}) copy-start(f32[5,24,128,128]{3,2,1,0:T(8,128)} %copy-done) | copy-start | bytes 23592964
Sparse Core Ops, SparseCore 0:
  8.9 47.9 all-gather.1

commit v5 on v4

--- a/solution.py
+++ b/solution.py
@@ -8,7 +8,7 @@
 from jax.sharding import PartitionSpec as P
 
 
-CHUNKS = 4
+CHUNKS = 8
 MESH = pl.DeviceIdType.MESH
 
 
@@ -120,12 +120,12 @@
         done, arrives = landing(d, p, k)
         pl.when(arrives)(done.wait_recv)
 
-    for k in (1, 0, 3, 2):
+    order = [k + 1 - 2 * (k % 2) for k in range(CHUNKS)]
+    for k in order:
         for d in range(2):
             send(d, 0, k)
     kept = pltpu.make_async_copy(own, win.at[2], kept_sem)
     kept.start()
-    order = (1, 0, 3, 2)
     for i in range(CHUNKS + 1):
         if i < CHUNKS:
             for d in range(2):

time: 171 us -> 174 us (1.018)
  Pallas kernels: 143 us -> 145 us
    pallas_call x1, Pallas kernels: 103 us -> 106 us  [gathered_window(): pl.pallas_call(functools.partial(window_kernel, rows, cols), out_shape=ja...]
  transfers between devices with their start and end apart: 1 -> 1, of which waited for: 0 -> 0; matrix products, arithmetic and copies ran while one was open for 2% -> 2% of each run, Pallas kernels for 60% -> 61%
where the time goes in v5:
time: 174 us
  Pallas kernels  145 us (83%)
  between operations  13.5 us (8%)
  local copies, waits for them, and re-layouts  11.9 us (7%)
  other arithmetic  2.1 us (1%)
    pallas_call x1, Pallas kernels, gathered_window(): pl.pallas_call(functools.partial(window_kernel, rows, cols), out_shape=ja...  106 us
    pallas_call x1, Pallas kernels, summed_shares(): pl.pallas_call(share_sum_kernel, out_shape=jax.ShapeDtypeStruct(kept, sha...  34.5 us
    unnamed x8, local copies, waits for them, and re-layouts  9.45 us
    pallas_call x1, Pallas kernels, products(): pl.pallas_call(products_kernel, out_shape=jax.ShapeDtypeStruct((rows, wan...  4.97 us
  transfers between devices with their start and end apart: 1, of which 0 were waited for; matrix products, arithmetic and copies ran while one was open for 2% of the time, Pallas kernels for 61%

profile of v5, /device:TPU:5, one launch (start us, length us, event | category | flops | bytes accessed | tf_op | source)
XLA Modules:
  0.0 173.6 jit_solution(16462589806393532924)
XLA Ops:
  6.5 0.0 all-gather.2.cloned.1.call-start
  6.5 0.7 all-gather.2.cloned.1.call-update
  7.3 0.8 copy.11
  8.1 0.8 fusion.2
  8.8 0.1 copy.12
  8.9 0.1 copy.10
  9.0 0.1 reshape.22
  9.1 0.6 gather_fusion
  9.7 1.2 select_reduce_fusion
  10.9 0.1 add_select_fusion
  11.0 0.1 select_n.33.table
  11.1 0.0 copy-start.2
  11.1 1.4 copy-done.2
  12.5 105.9 %shard_map.37 = f32[5,24,128,128]{3,2,1,0:T(8,128)S(1)} custom-call(f32[24,128,128]{2,1,0:T(8,128)S(1)} %bitcast.4), custom_call_target="tpu_custom_call" | custom-call | bytes 31457280 | tf_op jit(solution)/shard_map/pallas_call | solution.py:157
  118.4 0.0 copy-start
  118.4 3.1 %copy-done = f32[5,24,128,128]{3,2,1,0:T(8,128)} copy-done((f32[5,24,128,128]{3,2,1,0:T(8,128)}, f32[5,24,128,128]{3,2,1,0:T(8,128)S(1)}, u32[]{:S(2)}) %copy-start) | copy-done | bytes 7864344
  121.5 0.0 all-gather.2.cloned.1.call-done
  121.5 1.6 constant_dynamic-slice_fusion
  123.1 0.0 copy-start.1
  123.1 3.2 %copy-done.1 = f32[5,24,128,128]{3,2,1,0:T(8,128)S(1)} copy-done((f32[5,24,128,128]{3,2,1,0:T(8,128)S(1)}, f32[5,24,128,128]{3,2,1,0:T(8,128)}, u32[]{:S(2)}) %copy-start.1) | copy-done | bytes 7864344
  126.3 5.0 %shard_map.38.shares = f32[8,8,128,128]{3,2,1,0:T(8,128)S(1)} custom-call(s32[192]{0:T(256)S(1)} %select_n.33.table, f32[8,3,128,128]{3,2,1,0:T(8,128)S(1)} %bitcast.5, f32[120,128,128]{2,1,0:T(8,128)S(1)} %bitcast.3), custom_call_target="tpu_custom_call" | custom-call | flops 2415919104 | bytes 13631488 | tf_op jit(solution)/shard_map/pallas_call | solution.py:216
  131.3 34.5 %shard_map.39 = f32[2,8,128,128]{3,2,1,0:T(8,128)S(1)} custom-call(f32[8,8,128,128]{3,2,1,0:T(8,128)S(1)} %shard_map.38.shares), custom_call_target="tpu_custom_call" | custom-call | flops 1048576 | bytes 8388608 | tf_op jit(solution)/shard_map/pallas_call | solution.py:302
  165.7 1.0 copy.14
  (2 shorter events, 0.0 us)
Async XLA Ops:
  6.5 115.0 %all-gather.2.cloned.1.call-start = ((), (), s32[]{:S(2)}) async-start(), calls=%async_computation | async-start | bytes 7864320 | tf_op jit(solution)/shard_map/all_gather | solution.py:334
  11.1 1.4 copy-start.2
  118.4 3.1 %copy-start = (f32[5,24,128,128]{3,2,1,0:T(8,128)}, f32[5,24,128,128]{3,2,1,0:T(8,128)S(1)}, u32[]{:S(2)}) copy-start(f32[5,24,128,128]{3,2,1,0:T(8,128)S(1)} %shard_map.37) | copy-start | bytes 23592964
  123.1 3.2 %copy-start.1 = (f32[5,24,128,128]{3,2,1,0:T(8,128)S(1)}, f32[5,24,128,128]{3,2,1,0:T(8,128)}, u32[]{:S(2)}) copy-start(f32[5,24,128,128]{3,2,1,0:T(8,128)} %copy-done) | copy-start | bytes 23592964
Sparse Core Ops, SparseCore 0:
  8.9 47.9 all-gather.1

commit v6 on v4

--- a/solution.py
+++ b/solution.py
@@ -183,13 +183,13 @@
     return high, low
 
 
-def products_kernel(table, entries_ref, window_ref, out_ref):
+def products_kernel(table, layer, entries_ref, window_ref, out_ref):
     row = pl.program_id(0)
-    per_layer = entries_ref.shape[1]
+    per_layer = entries_ref.shape[2]
     wanted, order = out_ref.shape[1], out_ref.shape[3]
     left = []
     for s in range(per_layer):
-        a_high, a_low = two_part(entries_ref[0, s])
+        a_high, a_low = two_part(entries_ref[0, 0, s])
         left += [a_high, a_low, a_high]
     left = jnp.concatenate(left, axis=1)
     group = 2 if wanted % 2 == 0 else 1
@@ -211,27 +211,31 @@
             out_ref[0, first + at] = got[:, at * order : (at + 1) * order]
 
 
-def products(table, entries, window, wanted):
-    rows, per_layer, order, _ = entries.shape
+def products(table, layer, gathered, window, wanted):
+    row_count, layers, slot_total, order, _ = gathered.shape
+    rows, per_layer = row_count * layers, slot_total // layers
     return pl.pallas_call(
         products_kernel,
         out_shape=jax.ShapeDtypeStruct((rows, wanted, order, order), jnp.float32),
         grid_spec=pltpu.PrefetchScalarGridSpec(
-            num_scalar_prefetch=1,
+            num_scalar_prefetch=2,
             grid=(rows,),
             in_specs=[
-                pl.BlockSpec((1, per_layer, order, order), lambda r, t: (r, 0, 0, 0)),
-                pl.BlockSpec(window.shape, lambda r, t: (0, 0, 0)),
+                pl.BlockSpec(
+                    (1, 1, per_layer, order, order),
+                    lambda r, t, m: (r // layers, r % layers, m[0], 0, 0),
+                ),
+                pl.BlockSpec(window.shape, lambda r, t, m: (0, 0, 0)),
             ],
-            out_specs=pl.BlockSpec((1, wanted, order, order), lambda r, t: (r, 0, 0, 0)),
+            out_specs=pl.BlockSpec((1, wanted, order, order), lambda r, t, m: (r, 0, 0, 0)),
         ),
         compiler_params=pltpu.CompilerParams(vmem_limit_bytes=32 * 1024 * 1024),
         cost_estimate=pl.CostEstimate(
             flops=6 * rows * per_layer * wanted * order**3,
-            bytes_accessed=4 * (window.size + entries.size + rows * wanted * order * order),
+            bytes_accessed=4 * (window.size + gathered.size // layers + rows * wanted * order * order),
             transcendentals=0,
         ),
-    )(table, entries, window)
+    )(table, layer, gathered, window)
 
 
 PIECES = 2
@@ -332,8 +336,6 @@
     seg_rows = row_count * layers
     wanted = out_cols.shape[1]
     gathered = lax.all_gather(p_values, "rep", axis=1, tiled=True)
-    entries = lax.dynamic_slice_in_dim(gathered, layer_index * per_layer, per_layer, 2)
-    entries = entries.reshape(seg_rows, per_layer, order, order)
     window = gathered_window(own_rows.reshape(-1, order, order))
     window = window.reshape(-1, order, order)
     inner_cols = lax.dynamic_slice(
@@ -345,7 +347,7 @@
     slot_index = jnp.max(jnp.where(matches, slot_ids, -1), axis=3)
     window_idx = inner_cols // layers - (segment - 2) * row_count
     table = jnp.where(slot_index >= 0, window_idx[:, :, None] * slot_total + slot_index, -1)
-    shares = products(table.reshape(-1), entries, window, wanted)
+    shares = products(table.reshape(-1), layer_index.astype(jnp.int32)[None], gathered, window, wanted)
     return summed_shares(shares)
 
 

time: 171 us -> 173 us (1.012)
    unnamed x8 -> x10, local copies, waits for them, and re-layouts: 9.45 us -> 12.2 us
where the time goes in v6:
time: 173 us; the launch traced here: 172 us
  Pallas kernels  143 us (83%)
  between operations  13.5 us (8%)
  local copies, waits for them, and re-layouts  13.2 us (8%)
  other arithmetic  2.1 us (1%)
    pallas_call x1, Pallas kernels, gathered_window(): pl.pallas_call(functools.partial(window_kernel, rows, cols), out_shape=ja...  103 us
    pallas_call x1, Pallas kernels, summed_shares(): pl.pallas_call(share_sum_kernel, out_shape=jax.ShapeDtypeStruct(kept, sha...  34.9 us
    unnamed x10, local copies, waits for them, and re-layouts  12.2 us
    pallas_call x1, Pallas kernels, products(): pl.pallas_call(products_kernel, out_shape=jax.ShapeDtypeStruct((rows, wan...  5.02 us
  transfers between devices with their start and end apart: 1, of which 0 were waited for; matrix products, arithmetic and copies ran while one was open for 2% of the time, Pallas kernels for 60%

profile of v6, /device:TPU:5, one launch (start us, length us, event | category | flops | bytes accessed | tf_op | source)
XLA Modules:
  0.0 172.4 jit_solution(8156862363844572780)
XLA Ops:
  6.5 0.0 all-gather.2.cloned.1.call-start
  6.5 0.7 all-gather.2.cloned.1.call-update
  7.3 0.8 copy.11
  8.1 0.8 fusion.2
  8.8 0.1 copy.12
  8.9 0.1 copy.10
  9.0 0.1 reshape.18
  9.1 0.6 gather_fusion
  9.7 1.2 select_reduce_fusion
  10.9 0.1 add_select_fusion
  11.0 0.1 select_n.32.table
  11.1 0.0 copy-start.2
  11.1 1.4 copy-done.2
  12.5 103.0 %shard_map.37 = f32[5,24,128,128]{3,2,1,0:T(8,128)S(1)} custom-call(f32[24,128,128]{2,1,0:T(8,128)S(1)} %bitcast.4), custom_call_target="tpu_custom_call" | custom-call | bytes 31457280 | tf_op jit(solution)/shard_map/pallas_call | solution.py:157
  115.5 0.0 copy-start
  115.5 3.1 %copy-done = f32[5,24,128,128]{3,2,1,0:T(8,128)} copy-done((f32[5,24,128,128]{3,2,1,0:T(8,128)}, f32[5,24,128,128]{3,2,1,0:T(8,128)S(1)}, u32[]{:S(2)}) %copy-start) | copy-done | bytes 7864344
  118.6 0.0 all-gather.2.cloned.1.call-done.entries_ref
  118.6 0.0 copy-start.1
  118.6 3.2 %copy-done.1 = f32[5,24,128,128]{3,2,1,0:T(8,128)S(1)} copy-done((f32[5,24,128,128]{3,2,1,0:T(8,128)S(1)}, f32[5,24,128,128]{3,2,1,0:T(8,128)}, u32[]{:S(2)}) %copy-start.1) | copy-done | bytes 7864344
  121.8 0.0 copy-start.3
  121.8 2.8 %copy-done.3 = f32[2,4,12,128,128]{4,3,2,1,0:T(8,128)S(1)} copy-done((f32[2,4,12,128,128]{4,3,2,1,0:T(8,128)S(1)}, f32[2,4,12,128,128]{4,3,2,1,0:T(8,128)}, u32[]{:S(2)}) %copy-start.3) | copy-done | bytes 6291480
  124.6 5.0 %shard_map.38.shares = f32[8,8,128,128]{3,2,1,0:T(8,128)S(1)} custom-call(s32[192]{0:T(256)S(1)} %select_n.32.table, s32[1]{0:T(128)} %bitcast.layer, f32[2,4,12,128,128]{4,3,2,1,0:T(8,128)S(1)} %copy-done.3, f32[120,128,128]{2,1,0:T(8,128)S(1)} %bitcast.3), custom_call_target="tpu_custom_call" | custom-call | flops 2415919104 | bytes 13631488 | tf_op jit(solution)/shard_map/pallas_call | solution.py:217
  129.6 34.9 %shard_map.39 = f32[2,8,128,128]{3,2,1,0:T(8,128)S(1)} custom-call(f32[8,8,128,128]{3,2,1,0:T(8,128)S(1)} %shard_map.38.shares), custom_call_target="tpu_custom_call" | custom-call | flops 1048576 | bytes 8388608 | tf_op jit(solution)/shard_map/pallas_call | solution.py:306
  164.6 1.0 copy.14
  (2 shorter events, 0.0 us)
Async XLA Ops:
  6.5 112.0 %all-gather.2.cloned.1.call-start = ((), (), s32[]{:S(2)}) async-start(), calls=%async_computation | async-start | bytes 7864320 | tf_op jit(solution)/shard_map/all_gather | solution.py:338
  11.1 1.4 copy-start.2
  115.5 3.1 %copy-start = (f32[5,24,128,128]{3,2,1,0:T(8,128)}, f32[5,24,128,128]{3,2,1,0:T(8,128)S(1)}, u32[]{:S(2)}) copy-start(f32[5,24,128,128]{3,2,1,0:T(8,128)S(1)} %shard_map.37) | copy-start | bytes 23592964
  118.6 3.2 %copy-start.1 = (f32[5,24,128,128]{3,2,1,0:T(8,128)S(1)}, f32[5,24,128,128]{3,2,1,0:T(8,128)}, u32[]{:S(2)}) copy-start(f32[5,24,128,128]{3,2,1,0:T(8,128)} %copy-done) | copy-start | bytes 23592964
  121.8 2.8 %copy-start.3 = (f32[2,4,12,128,128]{4,3,2,1,0:T(8,128)S(1)}, f32[2,4,12,128,128]{4,3,2,1,0:T(8,128)}, u32[]{:S(2)}) copy-start(f32[2,4,12,128,128]{4,3,2,1,0:T(8,128)} %all-gather.2.cloned.1.call-done.entries_ref) | copy-start | bytes 18874372
Sparse Core Ops, SparseCore 0:
  8.9 47.9 all-gather.1
